TPU v7x, 128 devices: a whole 4x4x4 slice. The times are simulated.
128 devices in a mesh: blk: 128 (over x, y, z, core).
Axes of the slice: x: 4, y: 4, z: 4, core: 2. Of those that a mesh axis runs over, the one named last changes fastest.
Arguments:
- source_points: bfloat16 [49152, 256], P('blk')
- target_points: bfloat16 [131072, 256], P('blk')
- source_mass: float32 [49152], P('blk'), may hold values from 0.25 to 4
- target_mass: float32 [131072], P('blk'), may hold values from 0.25 to 4
- target_init: float32 [131072], P('blk'), may hold values from -1.8 to 1.8
- pair_tiles: int32 [16384, 2], P('blk'), may hold values from 0 to 7, as said below
- pair_count: int32 [16384], P('blk'), may hold values from 0 to 2, as said below
Outputs:
- source_pot: float32 [49152], P('blk')
- target_pot: float32 [131072], P('blk')
Inputs may be any that keep to these rules, and one draw needn't show every extreme that they name: `pair_tiles`: the entries of a row are distinct; entries past the row's count are padding, still tile numbers below 8. Every target tile is named by a valid entry of some row, and every source device has a valid entry in some row. `pair_count`: some rows hold 2 valid entries in every draw.
All inputs are finite; a program needn't handle non-finite values.
Results may differ from a plain program's by a relative error of at most 0.0003.
Values may be sent and summed in bfloat16 or wider, within the bound.
No kernel may reach another device: no remote copies, remote signals or barrier semaphores. Data moves between devices by JAX's collectives and lax.ppermute only.
A program may use at most 192 MiB of HBM per device.

v0:
```python
import functools
import math

import jax
import jax.numpy as jnp
import numpy as np
from jax import lax
from jax.experimental import pallas as pl
from jax.experimental.pallas import tpu as pltpu
from jax.sharding import Mesh
from jax.sharding import PartitionSpec as P

TSUB = 8
CAP = 2
ITERS = 2
EPSILON = 0.1

DIMS = (4, 4, 4, 2)
NAMES = ("x", "y", "z", "core")
ROWS = ("y", "z")
COLS = ("x", "core")
N_ROWS = 16
N_PIECES = 12
N_COLS = 8
RING = 4
SRC = 384
TILE = 128
SUBS = SRC // TILE
FEAT = 256
TILES = N_COLS * TSUB
SLOTS = N_ROWS * N_COLS * CAP
UNROLL = 16
LAST_UNROLL = 4
EXTRA = 16
LISTED = 8 + SLOTS + 4 * LAST_UNROLL
NOTHING = TILES << 8
NORMS = 16
GAIN = 2.0 / (FEAT * EPSILON)
UNIT = 1.0 / (FEAT * EPSILON)
LOG2E = math.log2(math.e)
SPAN = 70.0


def lse_over_first(parts):
    top = jnp.max(parts, axis=0)
    base = jnp.where(top == -jnp.inf, 0.0, top)
    return top + jnp.log(jnp.sum(jnp.exp(parts - base[None]), axis=0))


def spread(values, norm_ref):
    high, low = jnp.max(values), jnp.min(values)
    reach = GAIN * jnp.sqrt(jnp.max(norm_ref[0:8]) * jnp.max(norm_ref[8:16]))
    return 0.5 * high + 0.5 * low, 0.5 * high - 0.5 * low + reach <= SPAN


def diagonal():
    return lax.broadcasted_iota(jnp.int32, (TILE, TILE), 0) == lax.broadcasted_iota(
        jnp.int32, (TILE, TILE), 1
    )


def as_row(eye, col):
    return jnp.sum(jnp.where(eye, col, 0.0), axis=0, keepdims=True)


def as_col(eye, row):
    return jnp.sum(jnp.where(eye, row, 0.0), axis=1, keepdims=True)


def products(x, y):
    return jnp.dot(x, y, preferred_element_type=jnp.float32)


def item_at(item_ref, w):
    one, two = item_ref[8 + 2 * w], item_ref[9 + 2 * w]
    return (
        one >> 20,
        (one >> 16) & 15,
        (one >> 8) & 255,
        (two >> 8) & 255,
        one & 255,
        two & 255,
    )


def exps(x, y):
    return jnp.exp2((GAIN * LOG2E) * products(x, y))


def two_tiles(y_ref, r0, r1):
    return jnp.concatenate([y_ref[r0], y_ref[r1]], axis=1)


def sweep(n_items, work):
    def steps(first, size):
        def step(w, _):
            for k in range(size):
                work(first + size * w + k)
            return 0

        return step

    whole = lax.div(n_items, UNROLL)
    lax.fori_loop(0, whole, steps(0, UNROLL), 0)
    left = n_items - UNROLL * whole
    lax.fori_loop(
        0, lax.div(left + LAST_UNROLL - 1, LAST_UNROLL), steps(UNROLL * whole, LAST_UNROLL), 0
    )


def rescale(old, new):
    return jnp.where(old == new, 1.0, jnp.exp(old - new))


def split(values):
    high = values.astype(jnp.bfloat16).astype(jnp.float32)
    rest = values - high
    middle = rest.astype(jnp.bfloat16).astype(jnp.float32)
    return [high, middle, (rest - middle).astype(jnp.bfloat16).astype(jnp.float32)]


def start_all(pairs, sems):
    copies = [pltpu.make_async_copy(src, dst, sems.at[k]) for k, (src, dst) in enumerate(pairs)]
    for copy in copies:
        copy.start()
    return copies


def prepare_kernel(*refs):
    xo_ref, yo_ref, nx_ref, part_ref = refs[7:11]
    y_ref, mass_ref, goal_ref, init_ref, tile_ref, count_ref, sems = refs[11:]
    copies = start_all(
        zip(refs[:7], (xo_ref.at[0:SRC], y_ref, mass_ref, goal_ref, init_ref, tile_ref, count_ref)),
        sems,
    )
    eye = diagonal()
    for copy in copies[2:]:
        copy.wait()
    la = jnp.log(mass_ref[...])
    lb = jnp.log(goal_ref[...])

    copies[0].wait()
    norms = []
    for b in range(SUBS):
        x = xo_ref[b * TILE : (b + 1) * TILE, :].astype(jnp.float32)
        norms.append(as_row(eye, jnp.sum(x * x, axis=1, keepdims=True)))
    nx = jnp.concatenate(norms, axis=0)
    nx_ref[...] = nx
    bound = jnp.full((1, TILE), 1.01 * jnp.max(nx))
    left = split(la) + [bound, jnp.zeros((EXTRA - 10, TILE), jnp.float32)]
    right = [
        tile_ref[...].astype(jnp.float32),
        count_ref[...].astype(jnp.float32),
        jnp.zeros((EXTRA - 3, TILE), jnp.float32),
    ]
    extra = jnp.concatenate(
        [jnp.concatenate(left, axis=0), jnp.concatenate(right, axis=0)], axis=1
    )
    xo_ref[SRC:] = extra.astype(jnp.bfloat16)

    copies[1].wait()
    norms = []
    for t in range(TSUB):
        y = y_ref[t * TILE : (t + 1) * TILE, :].astype(jnp.float32).T
        norms.append(jnp.sum(y * y, axis=0, keepdims=True))
        yo_ref[t, 0:FEAT] = y.astype(jnp.bfloat16)
    ny = jnp.concatenate(norms, axis=0)
    part_ref[...] = EPSILON * (lb + UNIT * ny)
    a0 = init_ref[...] / EPSILON - ny * UNIT
    parts = split(a0) + split(lb)
    bound = jnp.full((1, TILE), 1.01 * jnp.max(ny))
    for t in range(TSUB):
        rows = [part[t : t + 1] for part in parts]
        rows += [bound, jnp.zeros((EXTRA - 7, TILE), jnp.float32)]
        yo_ref[t, FEAT:] = jnp.concatenate(rows, axis=0).astype(jnp.bfloat16)


def gray(k):
    return k ^ (k >> 1)


def ring_place(offset, first):
    place = gray(offset)
    other = ((place & 1) << 1) | (place >> 1)
    return jnp.where(first == 0, place, other)


def piece_copies(x_refs, y_refs, xs, ys, x_rows, y_rows):
    pairs = []
    for half in range(2):
        for later in range(RING):
            place = pl.ds(RING * later + 2 * half, 2)
            pairs.append((x_refs[RING * half + later].at[:, x_rows, :], xs.at[place]))
    start = 0
    for piece in y_refs:
        pairs.append((piece.at[:, y_rows, :], ys.at[pl.ds(start, piece.shape[0])]))
        start += piece.shape[0]
    return pairs


def first_kernel(*refs):
    at_ref, pieces = refs[0], refs[1 : 1 + N_PIECES]
    x_refs, y_refs = pieces[: 2 * RING], pieces[2 * RING :]
    out_ref, item_ref, cols_ref, rows_ref, xs, ys = refs[1 + N_PIECES : 7 + N_PIECES]
    a_buf, u_buf, acc, top, sems = refs[7 + N_PIECES : 12 + N_PIECES]
    a_ref, table, compact, numbers, x_extra, y_extra, small_sems, sem = refs[12 + N_PIECES :]
    la_ref, lb_ref = cols_ref.at[NORMS:], rows_ref.at[NORMS:]
    x, y, z, core = (at_ref[k] for k in range(4))

    small = start_all(
        piece_copies(
            x_refs, y_refs, x_extra, y_extra, slice(SRC, SRC + EXTRA), slice(FEAT, FEAT + EXTRA)
        ),
        small_sems,
    )
    large = start_all(
        piece_copies(x_refs, y_refs, xs, ys, slice(0, SRC), slice(0, FEAT)), sems
    )
    for copy in small:
        copy.wait()

    lane = lax.broadcasted_iota(jnp.int32, (CAP, TILE), 1)
    px, side = lane >> 5, lane & 1
    start = RING * (side ^ core) + ring_place(px ^ x, side)
    entry_base = ((TSUB * (2 * px + side)) << 8) + TSUB * start

    bound = None
    for later in range(RING):
        for sooner in range(RING):
            one, two = gray(sooner), gray(later)
            off_y = jnp.where(core == 0, one, two)
            off_z = jnp.where(core == 0, two, one)
            s = RING * (y ^ off_y) + (z ^ off_z)
            extra = x_extra[RING * later + sooner].astype(jnp.float32)
            la = extra[0:3, :TILE] + extra[3:6, :TILE] + extra[6:9, :TILE]
            for b in range(SUBS):
                la_ref[pl.ds(SUBS * s + b, 1), :] = la[b : b + 1]
            here = extra[9:10, :TILE]
            bound = here if bound is None else jnp.maximum(bound, here)
            numbers_here = extra[0:3, TILE:].astype(jnp.int32)
            head = (s << 20) | ((RING * later + sooner) << 16)
            entry = head | (entry_base + 257 * numbers_here[0:CAP])
            slot = lax.broadcasted_iota(jnp.int32, (CAP, TILE), 0)
            entry = jnp.where(slot < numbers_here[CAP : CAP + 1], entry, -1)
            for e in range(CAP):
                table[pl.ds(N_ROWS * e + s, 1), :] = entry[e : e + 1]
    for ref in (cols_ref, rows_ref):
        ref[0:8] = jnp.broadcast_to(bound, (8, TILE))

    lane = lax.broadcasted_iota(jnp.int32, (N_ROWS, TILE), 1) & (2 * N_ROWS - 1)
    moved = pltpu.roll(table[...], (TILE - 2 * (RING * y + z)) & (TILE - 1), axis=1)
    second = pltpu.roll(moved[N_ROWS:], 2, axis=1)
    compact[...] = jnp.where(lane < 2, moved[:N_ROWS], second)
    copy = pltpu.make_async_copy(compact, numbers, sem)
    copy.start()
    acc[...] = jnp.zeros_like(acc)

    bound = None
    for k in range(2 * RING):
        side = core ^ (k // RING)
        place = k % RING
        offset = jnp.where(side == 0, gray(place), (0, 3, 1, 2)[place])
        owner = 2 * (x ^ offset) + side
        extra = y_extra[TSUB * k : TSUB * (k + 1)].astype(jnp.float32)
        rows = pl.ds(pl.multiple_of(TSUB * owner, TSUB), TSUB)
        a_ref[rows, :] = extra[:, 0] + extra[:, 1] + extra[:, 2]
        lb_ref[rows, :] = extra[:, 3] + extra[:, 4] + extra[:, 5]
        here = extra[0, 6:7]
        bound = here if bound is None else jnp.maximum(bound, here)
    for ref in (cols_ref, rows_ref):
        ref[8:16] = jnp.broadcast_to(bound, (8, TILE))

    copy.wait()

    def block(s, place):
        for px in range(RING):
            for side in range(2):
                for e in range(CAP):
                    entry = numbers[s, 2 * N_ROWS * px + 2 * e + side]
                    item_ref[place] = entry
                    place = place + jnp.where(entry >= 0, 1, 0)
        item_ref[place] = jnp.int32(NOTHING)
        return place + (place & 1)

    end = lax.fori_loop(0, N_ROWS, block, jnp.int32(8))
    for k in range(2 * LAST_UNROLL):
        item_ref[end + k] = jnp.int32(NOTHING)
    item_ref[0] = (end - 8) >> 1
    item_ref[1] = RING * y + z
    for copy in large:
        copy.wait()
    row_core(a_ref[...], item_ref, xs, ys, cols_ref, out_ref, a_buf, u_buf, acc, top)


def row_kernel(item_ref, x_ref, y_ref, side_ref, parts_ref, out_ref, a_buf, u_buf, acc, top):
    acc[...] = jnp.zeros_like(acc)
    a = side_ref[NORMS:] - lse_over_first(parts_ref[...])
    row_core(a, item_ref, x_ref, y_ref, side_ref, out_ref, a_buf, u_buf, acc, top)


def row_core(a, item_ref, x_ref, y_ref, norm_ref, out_ref, a_buf, u_buf, acc, top):
    mid, fast = spread(a, norm_ref)
    n_items = item_ref[0]
    eye = diagonal()

    @pl.when(fast)
    def _():
        u_buf[0:TILES] = jnp.exp(a - mid)
        u_buf[TILES:] = jnp.zeros((8, TILE), jnp.float32)

        def work(w):
            s, h, t0, t1, r0, r1 = item_at(item_ref, w)
            u0, u1 = u_buf[pl.ds(t0, 1), :], u_buf[pl.ds(t1, 1), :]
            e = exps(x_ref[h], two_tiles(y_ref, r0, r1))
            acc[s] += e[:, :TILE] * u0 + e[:, TILE:] * u1

        sweep(n_items, work)
        for k in range(N_ROWS * SUBS):
            s, b = k // SUBS, k % SUBS
            col = jnp.sum(acc[s, b * TILE : (b + 1) * TILE, :], axis=1, keepdims=True)
            a_buf[k : k + 1, :] = as_row(eye, col)
        done = mid + jnp.log(a_buf[0 : N_ROWS * SUBS])
        out_ref[...] = jnp.broadcast_to(done[None], out_ref.shape)

    @pl.when(jnp.logical_not(fast))
    def _():
        a_buf[0:TILES] = a
        a_buf[TILES:] = jnp.zeros((8, TILE), jnp.float32)
        top[...] = jnp.full_like(top, -jnp.inf)

        def step(w, _):
            s, h, t0, t1, r0, r1 = item_at(item_ref, w)
            for t, r in ((t0, r0), (t1, r1)):

                @pl.when(t < TILES)
                def _(t=t, r=r):
                    score = GAIN * products(x_ref[h], y_ref[r]) + a_buf[pl.ds(t, 1), :]
                    old = top[s]
                    new = jnp.maximum(old, score)
                    acc[s] = acc[s] * rescale(old, new) + jnp.exp(score - new)
                    top[s] = new

            return 0

        lax.fori_loop(0, n_items, step, 0)

        def finish(k, _):
            s, b = lax.div(k, SUBS), lax.rem(k, SUBS)
            rows = pl.ds(pl.multiple_of(b * TILE, TILE), TILE)
            block = top[s, rows, :]
            high = jnp.max(block, axis=1, keepdims=True)
            base = jnp.where(high == -jnp.inf, 0.0, high)
            total = jnp.sum(acc[s, rows, :] * jnp.exp(block - base), axis=1, keepdims=True)
            high_row = jnp.max(jnp.where(eye, high, -jnp.inf), axis=0, keepdims=True)
            done = high_row + jnp.log(as_row(eye, total))
            out_ref[:, pl.ds(k, 1), :] = jnp.broadcast_to(done[None], (N_ROWS, 1, TILE))
            return 0

        lax.fori_loop(0, N_ROWS * SUBS, finish, 0)


def last_col_kernel(
    item_ref, x_ref, y_ref, side_ref, parts_ref, norm_ref, out_ref, f_ref, b_buf, *scratch
):
    b = side_ref[NORMS:] - lse_over_first(parts_ref[...])
    b_buf[...] = b
    for k in range(SUBS):
        here = b_buf[pl.ds(SUBS * item_ref[1] + k, 1), :]
        f_ref[k : k + 1, :] = EPSILON * (here + UNIT * norm_ref[k : k + 1, :])
    col_core(b, item_ref, x_ref, y_ref, side_ref, out_ref, *scratch)


def col_kernel(item_ref, x_ref, y_ref, side_ref, parts_ref, out_ref, *scratch):
    b = side_ref[NORMS:] - lse_over_first(parts_ref[...])
    col_core(b, item_ref, x_ref, y_ref, side_ref, out_ref, *scratch)


def col_core(b, item_ref, x_ref, y_ref, norm_ref, out_ref, spread_buf, acc, top):
    mid, fast = spread(b, norm_ref)
    n_items = item_ref[0]
    eye = diagonal()

    def lay_out(values):
        for k in range(N_ROWS * SUBS):
            s, part = k // SUBS, k % SUBS
            col = as_col(eye, values[k : k + 1, :])
            spread_buf[s, part * TILE : (part + 1) * TILE, :] = jnp.broadcast_to(col, (TILE, TILE))

    acc[...] = jnp.zeros_like(acc)

    @pl.when(fast)
    def _():
        lay_out(jnp.exp(b - mid))

        def work(w):
            s, h, t0, t1, r0, r1 = item_at(item_ref, w)
            e = exps(x_ref[h], two_tiles(y_ref, r0, r1))
            v = spread_buf[s]
            acc[t0] += jnp.sum((e[:, :TILE] * v).reshape(SRC // 8, 8, TILE), axis=0)
            acc[t1] += jnp.sum((e[:, TILE:] * v).reshape(SRC // 8, 8, TILE), axis=0)

        sweep(n_items, work)
        done = mid + jnp.log(jnp.sum(acc[0:TILES], axis=1))
        out_ref[...] = jnp.broadcast_to(done[None], out_ref.shape)

    @pl.when(jnp.logical_not(fast))
    def _():
        lay_out(b)
        top[...] = jnp.full_like(top, -jnp.inf)

        def step(w, _):
            s, h, t0, t1, r0, r1 = item_at(item_ref, w)
            for t, r in ((t0, r0), (t1, r1)):

                @pl.when(t < TILES)
                def _(t=t, r=r):
                    score = GAIN * products(x_ref[h], y_ref[r]) + spread_buf[s]
                    score = score.reshape(SRC // 8, 8, TILE)
                    old = top[t]
                    new = jnp.maximum(old, jnp.max(score, axis=0))
                    acc[t] = acc[t] * rescale(old, new) + jnp.sum(
                        jnp.exp(score - new[None]), axis=0
                    )
                    top[t] = new

            return 0

        lax.fori_loop(0, n_items, step, 0)
        high = jnp.max(top[0:TILES], axis=1)
        base = jnp.where(high == -jnp.inf, 0.0, high)
        total = jnp.sum(acc[0:TILES] * jnp.exp(top[0:TILES] - base[:, None, :]), axis=1)
        out_ref[...] = jnp.broadcast_to((high + jnp.log(total))[None], out_ref.shape)


VMEM = pl.BlockSpec(memory_space=pltpu.VMEM)
ANY = pl.BlockSpec(memory_space=pl.ANY)
SMEM = pl.BlockSpec(memory_space=pltpu.SMEM)


def limit(mebibytes):
    return pltpu.CompilerParams(vmem_limit_bytes=mebibytes * 1024 * 1024)


def shape(dims, dtype=jnp.float32):
    return jax.ShapeDtypeStruct(dims, dtype)


def prepare(*operands):
    return pl.pallas_call(
        prepare_kernel,
        out_shape=(
            shape((SRC + EXTRA, FEAT), jnp.bfloat16),
            shape((TSUB, FEAT + EXTRA, TILE), jnp.bfloat16),
            shape((SUBS, TILE)),
            shape((TSUB, TILE)),
        ),
        in_specs=[ANY] * 7,
        out_specs=(VMEM,) * 4,
        scratch_shapes=[
            pltpu.VMEM((TSUB * TILE, FEAT), jnp.bfloat16),
            pltpu.VMEM((SUBS, TILE), jnp.float32),
            pltpu.VMEM((TSUB, TILE), jnp.float32),
            pltpu.VMEM((TSUB, TILE), jnp.float32),
            pltpu.VMEM((CAP, TILE), jnp.int32),
            pltpu.VMEM((1, TILE), jnp.int32),
            pltpu.SemaphoreType.DMA((7,)),
        ],
        compiler_params=limit(60),
        name="prepare",
    )(*operands)


ROW_SCRATCH = [
    pltpu.VMEM((TILES + 8, TILE), jnp.float32),
    pltpu.VMEM((TILES + 8, TILE), jnp.float32),
    pltpu.VMEM((N_ROWS, SRC, TILE), jnp.float32),
    pltpu.VMEM((N_ROWS, SRC, TILE), jnp.float32),
]
COL_SCRATCH = [
    pltpu.VMEM((N_ROWS, SRC, TILE), jnp.float32),
    pltpu.VMEM((TILES + 1, 8, TILE), jnp.float32),
    pltpu.VMEM((TILES + 1, 8, TILE), jnp.float32),
]
ROW_PARTS = shape((N_ROWS, N_ROWS * SUBS, TILE))


def first_pass(at, pieces):
    return pl.pallas_call(
        first_kernel,
        out_shape=(
            ROW_PARTS,
            shape((LISTED,), jnp.int32),
            shape((NORMS + N_ROWS * SUBS, TILE)),
            shape((NORMS + TILES, TILE)),
            shape((N_ROWS, SRC, FEAT), jnp.bfloat16),
            shape((TILES, FEAT, TILE), jnp.bfloat16),
        ),
        in_specs=[SMEM] + [ANY] * N_PIECES,
        out_specs=(VMEM, SMEM, VMEM, VMEM, VMEM, VMEM),
        scratch_shapes=ROW_SCRATCH
        + [
            pltpu.SemaphoreType.DMA((N_PIECES,)),
            pltpu.VMEM((TILES, TILE), jnp.float32),
            pltpu.VMEM((CAP * N_ROWS, TILE), jnp.int32),
            pltpu.VMEM((N_ROWS, TILE), jnp.int32),
            pltpu.SMEM((N_ROWS, TILE), jnp.int32),
            pltpu.VMEM((N_ROWS, EXTRA, FEAT), jnp.bfloat16),
            pltpu.VMEM((TILES, EXTRA, TILE), jnp.bfloat16),
            pltpu.SemaphoreType.DMA((N_PIECES,)),
            pltpu.SemaphoreType.DMA,
        ],
        compiler_params=limit(24),
        name="first_row_pass",
    )(at, *[pltpu.with_memory_space_constraint(piece, pltpu.HBM) for piece in pieces])


def row_pass(items, *operands):
    return pl.pallas_call(
        row_kernel,
        out_shape=ROW_PARTS,
        in_specs=[SMEM] + [VMEM] * len(operands),
        out_specs=VMEM,
        scratch_shapes=ROW_SCRATCH,
        compiler_params=limit(20),
        name="row_pass",
    )(items, *operands)


def col_pass(items, *operands):
    return pl.pallas_call(
        col_kernel,
        out_shape=shape((N_COLS, TILES, TILE)),
        in_specs=[SMEM] + [VMEM] * len(operands),
        out_specs=VMEM,
        scratch_shapes=COL_SCRATCH,
        compiler_params=limit(20),
        name="col_pass",
    )(items, *operands)


def last_col_pass(items, *operands):
    return pl.pallas_call(
        last_col_kernel,
        out_shape=(shape((1, TILES, TILE)), shape((SUBS, TILE))),
        in_specs=[SMEM] + [VMEM] * len(operands),
        out_specs=(VMEM, VMEM),
        scratch_shapes=[pltpu.VMEM((N_ROWS * SUBS, TILE), jnp.float32)] + COL_SCRATCH,
        compiler_params=limit(20),
        name="last_col_pass",
    )(items, *operands)


def swap(blocks, axes):
    return lax.all_to_all(blocks, axes, split_axis=0, concat_axis=0, tiled=True)


def exchange(block, partner):
    pairs = []
    for place in range(N_ROWS * N_COLS):
        at = tuple(int(k) for k in np.unravel_index(place, DIMS))
        pairs.append((place, int(np.ravel_multi_index(partner(*at), DIMS))))
    return lax.ppermute(block, NAMES, pairs)


def doubled(block, partner):
    return jnp.concatenate([block, exchange(block, partner)])


def after(value, events):
    return lax.optimization_barrier((value, events))[0]


def gather_all(sources, targets):
    along = [source_partner(0, flip) for flip in (1, 3)]
    across = [source_partner(1, flip) for flip in (1, 3)]
    beside = [target_partner(order) for order in (0, 1)]

    pair = jnp.stack([sources, exchange(sources, along[0])])
    tiles = jnp.concatenate([targets, exchange(targets, beside[0])])
    other = exchange(pair, along[1])
    first, second = exchange(pair, across[0]), exchange(pair, across[1])
    further = exchange(after(tiles, pair), beside[1])
    relayed = exchange(first, across[1])
    pieces = [pair, first, second, relayed]
    near = exchange(after(tiles, first), sibling)
    first, second = exchange(other, across[0]), exchange(other, across[1])
    pieces += [other, first, second, exchange(second, across[0])]
    far = exchange(after(further, (relayed, first, pieces[-1])), sibling)
    return pieces + [tiles, further, near, far]


def source_partner(stage, flip):
    def partner(x, y, z, core):
        return (x, y ^ flip, z, core) if stage == core else (x, y, z ^ flip, core)

    return partner


def target_partner(order):
    return lambda x, y, z, core: (x ^ (1, 3)[order ^ core], y, z, core)


def sibling(x, y, z, core):
    return (x, y, z, core ^ 1)


def body(
    source_points, target_points, source_mass, target_mass, target_init, pair_tiles, pair_count
):
    x_block, y_block, source_norm, target_part = prepare(
        source_points,
        target_points,
        source_mass.reshape(SUBS, TILE),
        target_mass.reshape(TSUB, TILE),
        target_init.reshape(TSUB, TILE),
        pair_tiles.T,
        pair_count.reshape(1, -1),
    )
    pieces = gather_all(x_block, y_block)

    at = jnp.stack([lax.axis_index(name) for name in NAMES]).astype(jnp.int32)
    row_parts, items, cols, rows, xs, ys = first_pass(at, pieces)
    for iteration in range(ITERS - 1):
        col_parts = col_pass(items, xs, ys, cols, swap(row_parts, ROWS))
        row_parts = row_pass(items, xs, ys, rows, swap(col_parts, COLS))
    col_parts, source_pot = last_col_pass(
        items, xs, ys, cols, swap(row_parts, ROWS), source_norm
    )
    last = swap(col_parts.reshape(N_COLS, TSUB, TILE), COLS)
    target_pot = target_part - EPSILON * lse_over_first(last)
    return (source_pot.reshape(-1), target_pot.reshape(-1))


def solution(mesh):
    grid = Mesh(mesh.devices.reshape(DIMS), NAMES)
    placed = (
        P(NAMES, None),
        P(NAMES, None),
        P(NAMES),
        P(NAMES),
        P(NAMES),
        P(NAMES, None),
        P(NAMES),
    )
    return jax.shard_map(
        body, mesh=grid, in_specs=placed, out_specs=(P(NAMES), P(NAMES)), check_vma=False
    )
```

profile of v0, /device:TPU:1, one launch (start us, length us, event | category | flops | bytes accessed | tf_op | source)
XLA Modules:
  0.0 287.4 jit_solution(5705489614780270449)
XLA Ops:
  0.6 2.5 prepare.1
  3.1 3.4 %collective-permute-start.8 = (bf16[8,272,128]{2,1,0:T(8,128)(2,1)}, bf16[8,272,128]{2,1,0:T(8,128)(2,1)S(1)}, u32[]{:S(2)}, u32[]{:S(2)}) collective-permute-start(bf16[8,272,128]{2,1,0:T(8,128)(2,1)} %get-tuple-element.18), channel_id=1, source_target_pairs={{0,32},{1,97},{2,34},{3,99},{4,36},{5,101},{6,38},{7,103},{8,40},{... | collective-permute-start | bytes 1671176 | tf_op jit(solution)/shard_map/ppermute | solution.py:562
  6.5 1.6 collective-permute-start
  8.2 1.1 constant_dynamic-update-slice_fusion.1
  9.3 2.6 collective-permute-done
  11.9 3.7 %collective-permute-start.4 = (bf16[2,400,256]{2,1,0:T(8,128)(2,1)S(1)}, bf16[2,400,256]{2,1,0:T(8,128)(2,1)S(1)}, u32[]{:S(2)}, u32[]{:S(2)}) collective-permute-start(bf16[2,400,256]{2,1,0:T(8,128)(2,1)S(1)} %pad_maximum_fusion.refs_1_), channel_id=1, source_target_pairs={{0,24},{1,7},{2,26},{3,5},{4,28},{5,3},{6,30},{7,1},{8,16},{9,15},... | collective-permute-start | bytes 1228808 | tf_op jit(solution)/shard_map/ppermute | solution.py:562
  15.5 0.0 collective-permute-done.8
  15.5 0.1 constant_dynamic-update-slice_fusion.refs_9_
  15.6 0.1 collective-permute-start.9
  15.7 1.4 collective-permute-start.1
  17.1 4.1 %collective-permute-done.4.refs_5_ = bf16[2,400,256]{2,1,0:T(8,128)(2,1)S(1)} collective-permute-done((bf16[2,400,256]{2,1,0:T(8,128)(2,1)S(1)}, bf16[2,400,256]{2,1,0:T(8,128)(2,1)S(1)}, u32[]{:S(2)}, u32[]{:S(2)}) %collective-permute-start.4) | collective-permute-done | bytes 409632 | tf_op jit(solution)/shard_map/ppermute | solution.py:562
  21.2 2.7 collective-permute-start.6
  23.9 1.7 collective-permute-start.3
  25.6 3.9 %collective-permute-done.6.refs_7_ = bf16[2,400,256]{2,1,0:T(8,128)(2,1)S(1)} collective-permute-done((bf16[2,400,256]{2,1,0:T(8,128)(2,1)S(1)}, bf16[2,400,256]{2,1,0:T(8,128)(2,1)S(1)}, u32[]{:S(2)}, u32[]{:S(2)}) %collective-permute-start.6) | collective-permute-done | bytes 409632 | tf_op jit(solution)/shard_map/ppermute | solution.py:562
  29.5 0.0 collective-permute-start.7
  29.6 1.9 collective-permute-start.10
  31.5 0.0 collective-permute-done.5.refs_6_
  31.5 2.5 collective-permute-done.3.refs_4_
  33.9 2.7 collective-permute-done.7.refs_8_
  36.7 2.8 collective-permute-start.11
  39.5 2.7 collective-permute-start.2
  42.3 0.1 pad_add_fusion.refs_0_
  42.3 5.7 %collective-permute-done.2.refs_3_ = bf16[2,400,256]{2,1,0:T(8,128)(2,1)} collective-permute-done((bf16[2,400,256]{2,1,0:T(8,128)(2,1)S(1)}, bf16[2,400,256]{2,1,0:T(8,128)(2,1)}, u32[]{:S(2)}, u32[]{:S(2)}) %collective-permute-start.2) | collective-permute-done | bytes 409632 | tf_op jit(solution)/shard_map/ppermute | solution.py:562
  48.0 48.4 %first_row_pass.1 = (f32[16,48,128]{2,1,0:T(8,128)S(1)}, s32[280]{0:T(512)S(1)}, f32[64,128]{1,0:T(8,128)S(1)}, f32[80,128]{1,0:T(8,128)S(1)}, bf16[16,384,256]{...) custom-call(s32[4]{0:T(128)S(1)} %pad_add_fusion.refs_0_, bf16[2,400,256]{2,1,0:T(8,128)(2,1)} %copy-done.2, ...), custom_call_target="tpu_custom_call" | custom-call | tf_op jit(solution)/shard_map/first_row_pass/pallas_call | solution.py:488
  96.5 20.1 %all_to_all.20.parts_ref = f32[16,48,128]{2,1,0:T(8,128)S(1)} all-to-all(f32[16,48,128]{2,1,0:T(8,128)S(1)} %get-tuple-element.27), channel_id=1, replica_groups=mesh['x'=4,'y'=4,'z'=4,'core'=2] {'y','z'}, dimensions={0} | all-to-all | bytes 786432 | tf_op jit(solution)/shard_map/all_to_all | solution.py:554
  116.6 37.5 %col_pass.1 = f32[8,64,128]{2,1,0:T(8,128)S(1)} custom-call(s32[280]{0:T(512)S(1)} %get-tuple-element.22.item_ref, bf16[16,384,256]{2,1,0:T(8,128)(2,1)S(1)} %get-tuple-element.23.x_ref, bf16[64,256,128]{2,1,0:T(8,128)(2,1)S(1)} %get-tuple-element.24.y_ref, f32[64,128]{1,0:T(8,128)S(1)} %get-tuple-element.25.side_ref, f32[16,48,128]{2,1,0:T(8,128)S(1)} %all_to_all.20.parts_ref), custom_call_target="tpu_custom_call" | custom-call | tf_op jit(solution)/shard_map/col_pass/pallas_call | solution.py:530
  154.1 15.4 %all_to_all.21.parts_ref = f32[8,64,128]{2,1,0:T(8,128)S(1)} all-to-all(f32[8,64,128]{2,1,0:T(8,128)S(1)} %col_pass.1), channel_id=1, replica_groups=mesh['x'=4,'y'=4,'z'=4,'core'=2] {'x','core'}, dimensions={0} | all-to-all | bytes 524288 | tf_op jit(solution)/shard_map/all_to_all | solution.py:554
  169.5 43.3 %row_pass.1 = f32[16,48,128]{2,1,0:T(8,128)S(1)} custom-call(s32[280]{0:T(512)S(1)} %get-tuple-element.22.item_ref, bf16[16,384,256]{2,1,0:T(8,128)(2,1)S(1)} %get-tuple-element.23.x_ref, bf16[64,256,128]{2,1,0:T(8,128)(2,1)S(1)} %get-tuple-element.24.y_ref, f32[80,128]{1,0:T(8,128)S(1)} %get-tuple-element.26.side_ref, f32[8,64,128]{2,1,0:T(8,128)S(1)} %all_to_all.21.parts_ref), custom_call_target="tpu_custom_call" | custom-call | tf_op jit(solution)/shard_map/row_pass/pallas_call | solution.py:518
  212.8 18.4 %all_to_all.22.parts_ref = f32[16,48,128]{2,1,0:T(8,128)S(1)} all-to-all(f32[16,48,128]{2,1,0:T(8,128)S(1)} %row_pass.1), channel_id=1, replica_groups=mesh['x'=4,'y'=4,'z'=4,'core'=2] {'y','z'}, dimensions={0} | all-to-all | bytes 786432 | tf_op jit(solution)/shard_map/all_to_all | solution.py:554
  231.2 38.1 %last_col_pass.1 = (f32[1,64,128]{2,1,0:T(8,128)S(1)}, f32[3,128]{1,0:T(4,128)}) custom-call(s32[280]{0:T(512)S(1)} %get-tuple-element.22.item_ref, bf16[16,384,256]{2,1,0:T(8,128)(2,1)S(1)} %get-tuple-element.23.x_ref, bf16[64,256,128]{2,1,0:T(8,128)(2,1)S(1)} %get-tuple-element.24.y_ref, f32[64,128]{1,0:T(8,128)S(1)} %get-tuple-element.25.side_ref, ...), custom_call_target="tpu_custom_call" | custom-call | tf_op jit(solution)/shard_map/last_col_pass/pallas_call | solution.py:542
  269.3 17.5 %all_to_all.23 = f32[8,8,128]{2,1,0:T(8,128)S(1)} all-to-all(f32[8,8,128]{2,1,0:T(8,128)S(1)} %bitcast.15), channel_id=1, replica_groups=mesh['x'=4,'y'=4,'z'=4,'core'=2] {'x','core'}, dimensions={0} | all-to-all | bytes 65536 | tf_op jit(solution)/shard_map/all_to_all | solution.py:554
  286.8 0.6 subtract_bitcast_fusion
  (33 shorter events, 0.1 us)
Async XLA Ops:
  3.1 8.7 %copy-start.10 = (bf16[400,256]{1,0:T(8,128)(2,1)S(1)}, bf16[400,256]{1,0:T(8,128)(2,1)}, u32[]{:S(2)}) copy-start(bf16[400,256]{1,0:T(8,128)(2,1)} %get-tuple-element.17) | copy-start | bytes 614404
  3.1 12.4 %collective-permute-start.8 = (bf16[8,272,128]{2,1,0:T(8,128)(2,1)}, bf16[8,272,128]{2,1,0:T(8,128)(2,1)S(1)}, u32[]{:S(2)}, u32[]{:S(2)}) collective-permute-start(bf16[8,272,128]{2,1,0:T(8,128)(2,1)} %get-tuple-element.18), channel_id=1, source_target_pairs={{0,32},{1,97},{2,34},{3,99},{4,36},{5,101},{6,38},{7,103},{8,40},{... | collective-permute-start | bytes 1671176 | tf_op jit(solution)/shard_map/ppermute | solution.py:562
  6.5 5.3 %collective-permute-start = (bf16[400,256]{1,0:T(8,128)(2,1)}, bf16[400,256]{1,0:T(8,128)(2,1)S(1)}, u32[]{:S(2)}, u32[]{:S(2)}) collective-permute-start(bf16[400,256]{1,0:T(8,128)(2,1)} %get-tuple-element.17), channel_id=1, source_target_pairs={{0,8},{1,3},{2,10},{3,1},{4,12},{5,7},{6,14},{7,5},{8,0},{9,11},{1... | collective-permute-start | bytes 614408 | tf_op jit(solution)/shard_map/ppermute | solution.py:562
  11.9 36.1 %copy-start.2 = (bf16[2,400,256]{2,1,0:T(8,128)(2,1)}, bf16[2,400,256]{2,1,0:T(8,128)(2,1)S(1)}, u32[]{:S(2)}) copy-start(bf16[2,400,256]{2,1,0:T(8,128)(2,1)S(1)} %pad_maximum_fusion.refs_1_) | copy-start | bytes 1228804
  11.9 9.3 %collective-permute-start.4 = (bf16[2,400,256]{2,1,0:T(8,128)(2,1)S(1)}, bf16[2,400,256]{2,1,0:T(8,128)(2,1)S(1)}, u32[]{:S(2)}, u32[]{:S(2)}) collective-permute-start(bf16[2,400,256]{2,1,0:T(8,128)(2,1)S(1)} %pad_maximum_fusion.refs_1_), channel_id=1, source_target_pairs={{0,24},{1,7},{2,26},{3,5},{4,28},{5,3},{6,30},{7,1},{8,16},{9,15},... | collective-permute-start | bytes 1228808 | tf_op jit(solution)/shard_map/ppermute | solution.py:562
  15.6 32.4 %copy-start.1 = (bf16[16,272,128]{2,1,0:T(8,128)(2,1)}, bf16[16,272,128]{2,1,0:T(8,128)(2,1)S(1)}, u32[]{:S(2)}) copy-start(bf16[16,272,128]{2,1,0:T(8,128)(2,1)S(1)} %constant_dynamic-update-slice_fusion.refs_9_) | copy-start | bytes 3342340
  15.6 21.0 %collective-permute-start.9 = (bf16[16,272,128]{2,1,0:T(8,128)(2,1)S(1)}, bf16[16,272,128]{2,1,0:T(8,128)(2,1)S(1)}, u32[]{:S(2)}, u32[]{:S(2)}) collective-permute-start(bf16[16,272,128]{2,1,0:T(8,128)(2,1)S(1)} %constant_dynamic-update-slice_fusion.refs_9_), channel_id=1, source_target_pairs={{0,96},{1,33},{2,98},{3,35},{4,100},{5,37},{6,102},{7,39},{8,104},... | collective-permute-start | bytes 3342344 | tf_op jit(solution)/shard_map/ppermute | solution.py:562
  15.7 8.2 %collective-permute-start.1 = (bf16[2,400,256]{2,1,0:T(8,128)(2,1)S(1)}, bf16[2,400,256]{2,1,0:T(8,128)(2,1)S(1)}, u32[]{:S(2)}, u32[]{:S(2)}) collective-permute-start(bf16[2,400,256]{2,1,0:T(8,128)(2,1)S(1)} %pad_maximum_fusion.refs_1_), channel_id=1, source_target_pairs={{0,2},{1,9},{2,0},{3,11},{4,6},{5,13},{6,4},{7,15},{8,10},{9,1},{1... | collective-permute-start | bytes 1228808 | tf_op jit(solution)/shard_map/ppermute | solution.py:562
  21.2 26.8 %copy-start.4 = (bf16[2,400,256]{2,1,0:T(8,128)(2,1)}, bf16[2,400,256]{2,1,0:T(8,128)(2,1)S(1)}, u32[]{:S(2)}) copy-start(bf16[2,400,256]{2,1,0:T(8,128)(2,1)S(1)} %collective-permute-done.4.refs_5_) | copy-start | bytes 1228804
  21.2 8.4 %collective-permute-start.6 = (bf16[2,400,256]{2,1,0:T(8,128)(2,1)S(1)}, bf16[2,400,256]{2,1,0:T(8,128)(2,1)S(1)}, u32[]{:S(2)}, u32[]{:S(2)}) collective-permute-start(bf16[2,400,256]{2,1,0:T(8,128)(2,1)S(1)} %collective-permute-done.4.refs_5_), channel_id=1, source_target_pairs={{0,6},{1,25},{2,4},{3,27},{4,2},{5,29},{6,0},{7,31},{8,14},{9,17},... | collective-permute-start | bytes 1228808 | tf_op jit(solution)/shard_map/ppermute | solution.py:562
  23.9 7.6 %collective-permute-start.5 = (bf16[2,400,256]{2,1,0:T(8,128)(2,1)S(1)}, bf16[2,400,256]{2,1,0:T(8,128)(2,1)S(1)}, u32[]{:S(2)}, u32[]{:S(2)}) collective-permute-start(bf16[2,400,256]{2,1,0:T(8,128)(2,1)S(1)} %collective-permute-done.4.refs_5_), channel_id=1, source_target_pairs={{0,2},{1,9},{2,0},{3,11},{4,6},{5,13},{6,4},{7,15},{8,10},{9,1},{1... | collective-permute-start | bytes 1228808 | tf_op jit(solution)/shard_map/ppermute | solution.py:562
  23.9 24.1 %copy-start.5 = (bf16[2,400,256]{2,1,0:T(8,128)(2,1)}, bf16[2,400,256]{2,1,0:T(8,128)(2,1)S(1)}, u32[]{:S(2)}) copy-start(bf16[2,400,256]{2,1,0:T(8,128)(2,1)S(1)} %collective-permute-done.1.refs_2_) | copy-start | bytes 1228804
  23.9 10.0 %collective-permute-start.3 = (bf16[2,400,256]{2,1,0:T(8,128)(2,1)S(1)}, bf16[2,400,256]{2,1,0:T(8,128)(2,1)S(1)}, u32[]{:S(2)}, u32[]{:S(2)}) collective-permute-start(bf16[2,400,256]{2,1,0:T(8,128)(2,1)S(1)} %collective-permute-done.1.refs_2_), channel_id=1, source_target_pairs={{0,6},{1,25},{2,4},{3,27},{4,2},{5,29},{6,0},{7,31},{8,14},{9,17},... | collective-permute-start | bytes 1228808 | tf_op jit(solution)/shard_map/ppermute | solution.py:562
  29.5 7.1 %copy-start.6 = (bf16[2,400,256]{2,1,0:T(8,128)(2,1)}, bf16[2,400,256]{2,1,0:T(8,128)(2,1)S(1)}, u32[]{:S(2)}) copy-start(bf16[2,400,256]{2,1,0:T(8,128)(2,1)S(1)} %collective-permute-done.6.refs_7_) | copy-start | bytes 1228804
  29.5 7.1 %collective-permute-start.7 = (bf16[2,400,256]{2,1,0:T(8,128)(2,1)S(1)}, bf16[2,400,256]{2,1,0:T(8,128)(2,1)S(1)}, u32[]{:S(2)}, u32[]{:S(2)}) collective-permute-start(bf16[2,400,256]{2,1,0:T(8,128)(2,1)S(1)} %collective-permute-done.6.refs_7_), channel_id=1, source_target_pairs={{0,2},{1,9},{2,0},{3,11},{4,6},{5,13},{6,4},{7,15},{8,10},{9,1},{1... | collective-permute-start | bytes 1228808 | tf_op jit(solution)/shard_map/ppermute | solution.py:562
  29.6 18.4 %collective-permute-start.10 = (bf16[16,272,128]{2,1,0:T(8,128)(2,1)S(1)}, bf16[16,272,128]{2,1,0:T(8,128)(2,1)}, u32[]{:S(2)}, u32[]{:S(2)}) collective-permute-start(bf16[16,272,128]{2,1,0:T(8,128)(2,1)S(1)} %constant_dynamic-update-slice_fusion.refs_9_), channel_id=1, source_target_pairs={{0,1},{1,0},{2,3},{3,2},{4,5},{5,4},{6,7},{7,6},{8,9},{9,8},{10,11... | collective-permute-start | bytes 3342344 | tf_op jit(solution)/shard_map/ppermute | solution.py:562
  31.5 8.0 %copy-start.7 = (bf16[2,400,256]{2,1,0:T(8,128)(2,1)}, bf16[2,400,256]{2,1,0:T(8,128)(2,1)S(1)}, u32[]{:S(2)}) copy-start(bf16[2,400,256]{2,1,0:T(8,128)(2,1)S(1)} %collective-permute-done.5.refs_6_) | copy-start | bytes 1228804
  33.9 8.3 %copy-start.8 = (bf16[2,400,256]{2,1,0:T(8,128)(2,1)}, bf16[2,400,256]{2,1,0:T(8,128)(2,1)S(1)}, u32[]{:S(2)}) copy-start(bf16[2,400,256]{2,1,0:T(8,128)(2,1)S(1)} %collective-permute-done.3.refs_4_) | copy-start | bytes 1228804
  36.6 5.6 %copy-start.9 = (bf16[2,400,256]{2,1,0:T(8,128)(2,1)}, bf16[2,400,256]{2,1,0:T(8,128)(2,1)S(1)}, u32[]{:S(2)}) copy-start(bf16[2,400,256]{2,1,0:T(8,128)(2,1)S(1)} %collective-permute-done.7.refs_8_) | copy-start | bytes 1228804
  36.7 11.4 %copy-start.3 = (bf16[16,272,128]{2,1,0:T(8,128)(2,1)}, bf16[16,272,128]{2,1,0:T(8,128)(2,1)S(1)}, u32[]{:S(2)}) copy-start(bf16[16,272,128]{2,1,0:T(8,128)(2,1)S(1)} %collective-permute-done.9.refs_10_) | copy-start | bytes 3342340
  36.7 11.3 %collective-permute-start.11 = (bf16[16,272,128]{2,1,0:T(8,128)(2,1)S(1)}, bf16[16,272,128]{2,1,0:T(8,128)(2,1)}, u32[]{:S(2)}, u32[]{:S(2)}) collective-permute-start(bf16[16,272,128]{2,1,0:T(8,128)(2,1)S(1)} %collective-permute-done.9.refs_10_), channel_id=1, source_target_pairs={{0,1},{1,0},{2,3},{3,2},{4,5},{5,4},{6,7},{7,6},{8,9},{9,8},{10,11... | collective-permute-start | bytes 3342344 | tf_op jit(solution)/shard_map/ppermute | solution.py:562
  39.5 8.5 %collective-permute-start.2 = (bf16[2,400,256]{2,1,0:T(8,128)(2,1)S(1)}, bf16[2,400,256]{2,1,0:T(8,128)(2,1)}, u32[]{:S(2)}, u32[]{:S(2)}) collective-permute-start(bf16[2,400,256]{2,1,0:T(8,128)(2,1)S(1)} %pad_maximum_fusion.refs_1_), channel_id=1, source_target_pairs={{0,6},{1,25},{2,4},{3,27},{4,2},{5,29},{6,0},{7,31},{8,14},{9,17},... | collective-permute-start | bytes 1228808 | tf_op jit(solution)/shard_map/ppermute | solution.py:562
  169.5 61.7 %copy-start = (f32[3,128]{1,0:T(4,128)S(1)}, f32[3,128]{1,0:T(4,128)}, u32[]{:S(2)}) copy-start(f32[3,128]{1,0:T(4,128)} %get-tuple-element.28.norm_ref) | copy-start | bytes 4612
  231.2 55.6 %copy-start.11 = (f32[8,128]{1,0:T(8,128)S(1)}, f32[8,128]{1,0:T(8,128)}, u32[]{:S(2)}) copy-start(f32[8,128]{1,0:T(8,128)} %get-tuple-element.30) | copy-start | bytes 12292
where the time goes:
time: 286 us; the launch traced here: 287 us
  Pallas kernels  170 us (59%)
  blocking collectives  71.4 us (25%)
  starting transfers between devices  22.1 us (8%)
  waiting for transfers between devices  21.4 us (7%)
    all_to_all x4, blocking collectives, swap(): return lax.all_to_all(blocks, axes, split_axis=0, concat_axis=0, tiled=True)  71.4 us
    pallas_call x1, Pallas kernels, first_pass(): pl.pallas_call(first_kernel, out_shape=(ROW_PARTS, shape((LISTED,), jnp.i...  48.4 us
    pallas_call x1, Pallas kernels, row_pass(): pl.pallas_call(row_kernel, out_shape=ROW_PARTS, in_specs=[SMEM] + [VMEM]...  43.3 us
    pallas_call x1, Pallas kernels, last_col_pass(): pl.pallas_call(last_col_kernel, out_shape=(shape((1, TILES, TILE)), shape...  38.1 us
    pallas_call x1, Pallas kernels, col_pass(): pl.pallas_call(col_kernel, out_shape=shape((N_COLS, TILES, TILE)), in_spe...  37.5 us
    ppermute x12, starting transfers between devices, exchange(): return lax.ppermute(block, NAMES, pairs)  22.1 us
    ppermute x12, waiting for transfers between devices, exchange(): return lax.ppermute(block, NAMES, pairs)  21.4 us
  transfers between devices with their start and end apart: 12, of which 6 were waited for; matrix products, arithmetic and copies ran while one was open for 0% of the time, Pallas kernels for 0%

commit v1 on v0

--- a/solution.py
+++ b/solution.py
@@ -100,12 +100,13 @@
 
         return step
 
-    whole = lax.div(n_items, UNROLL)
-    lax.fori_loop(0, whole, steps(0, UNROLL), 0)
-    left = n_items - UNROLL * whole
-    lax.fori_loop(
-        0, lax.div(left + LAST_UNROLL - 1, LAST_UNROLL), steps(UNROLL * whole, LAST_UNROLL), 0
-    )
+    done = 0
+    for size in (UNROLL, UNROLL // 2):
+        whole = lax.div(n_items - done, size)
+        lax.fori_loop(0, whole, steps(done, size), 0)
+        done = done + size * whole
+    left = lax.div(n_items - done + LAST_UNROLL - 1, LAST_UNROLL)
+    lax.fori_loop(0, left, steps(done, LAST_UNROLL), 0)
 
 
 def rescale(old, new):
@@ -582,7 +583,7 @@
     further = exchange(after(tiles, pair), beside[1])
     relayed = exchange(first, across[1])
     pieces = [pair, first, second, relayed]
-    near = exchange(after(tiles, first), sibling)
+    near = exchange(after(tiles, (first, second)), sibling)
     first, second = exchange(other, across[0]), exchange(other, across[1])
     pieces += [other, first, second, exchange(second, across[0])]
     far = exchange(after(further, (relayed, first, pieces[-1])), sibling)

time: 286 us -> 279 us (0.976)
  blocking collectives: 71.4 us -> 63.6 us
  Pallas kernels: 170 us -> 175 us
    all_to_all x4, blocking collectives: 71.4 us -> 63.6 us  [swap(): return lax.all_to_all(blocks, axes, split_axis=0, concat_axis=0, tiled=True)]
where the time goes in v1:
time: 279 us; the launch traced here: 280 us
  Pallas kernels  175 us (63%)
  blocking collectives  63.6 us (23%)
  starting transfers between devices  19.6 us (7%)
  waiting for transfers between devices  18.8 us (7%)
    all_to_all x4, blocking collectives, swap(): return lax.all_to_all(blocks, axes, split_axis=0, concat_axis=0, tiled=True)  63.6 us
    pallas_call x1, Pallas kernels, first_pass(): pl.pallas_call(first_kernel, out_shape=(ROW_PARTS, shape((LISTED,), jnp.i...  49.7 us
    pallas_call x1, Pallas kernels, row_pass(): pl.pallas_call(row_kernel, out_shape=ROW_PARTS, in_specs=[SMEM] + [VMEM]...  44.4 us
    pallas_call x1, Pallas kernels, last_col_pass(): pl.pallas_call(last_col_kernel, out_shape=(shape((1, TILES, TILE)), shape...  39.5 us
    pallas_call x1, Pallas kernels, col_pass(): pl.pallas_call(col_kernel, out_shape=shape((N_COLS, TILES, TILE)), in_spe...  39.1 us
    ppermute x12, starting transfers between devices, exchange(): return lax.ppermute(block, NAMES, pairs)  19.6 us
    ppermute x12, waiting for transfers between devices, exchange(): return lax.ppermute(block, NAMES, pairs)  18.8 us
  transfers between devices with their start and end apart: 12, of which 6 were waited for; matrix products, arithmetic and copies ran while one was open for 0% of the time, Pallas kernels for 0%

profile of v1, /device:TPU:1, one launch (start us, length us, event | category | flops | bytes accessed | tf_op | source)
XLA Modules:
  0.0 279.8 jit_solution(14444726082427281712)
XLA Ops:
  0.6 2.5 prepare.1
  3.1 3.4 %collective-permute-start.8 = (bf16[8,272,128]{2,1,0:T(8,128)(2,1)}, bf16[8,272,128]{2,1,0:T(8,128)(2,1)S(1)}, u32[]{:S(2)}, u32[]{:S(2)}) collective-permute-start(bf16[8,272,128]{2,1,0:T(8,128)(2,1)} %get-tuple-element.18), channel_id=1, source_target_pairs={{0,32},{1,97},{2,34},{3,99},{4,36},{5,101},{6,38},{7,103},{8,40},{... | collective-permute-start | bytes 1671176 | tf_op jit(solution)/shard_map/ppermute | solution.py:563
  6.5 1.6 collective-permute-start
  8.2 1.1 constant_dynamic-update-slice_fusion.1
  9.3 2.6 collective-permute-done
  11.9 3.7 %collective-permute-start.4 = (bf16[2,400,256]{2,1,0:T(8,128)(2,1)S(1)}, bf16[2,400,256]{2,1,0:T(8,128)(2,1)S(1)}, u32[]{:S(2)}, u32[]{:S(2)}) collective-permute-start(bf16[2,400,256]{2,1,0:T(8,128)(2,1)S(1)} %pad_maximum_fusion.refs_1_), channel_id=1, source_target_pairs={{0,24},{1,7},{2,26},{3,5},{4,28},{5,3},{6,30},{7,1},{8,16},{9,15},... | collective-permute-start | bytes 1228808 | tf_op jit(solution)/shard_map/ppermute | solution.py:563
  15.5 0.1 constant_dynamic-update-slice_fusion.refs_9_
  15.6 0.1 collective-permute-start.9
  15.7 1.4 collective-permute-start.1
  17.1 4.1 %collective-permute-done.4.refs_5_ = bf16[2,400,256]{2,1,0:T(8,128)(2,1)S(1)} collective-permute-done((bf16[2,400,256]{2,1,0:T(8,128)(2,1)S(1)}, bf16[2,400,256]{2,1,0:T(8,128)(2,1)S(1)}, u32[]{:S(2)}, u32[]{:S(2)}) %collective-permute-start.4) | collective-permute-done | bytes 409632 | tf_op jit(solution)/shard_map/ppermute | solution.py:563
  21.2 2.7 collective-permute-start.6
  23.9 0.0 collective-permute-start.2
  24.0 2.7 collective-permute-start.3
  26.7 2.9 %collective-permute-done.6.refs_7_ = bf16[2,400,256]{2,1,0:T(8,128)(2,1)S(1)} collective-permute-done((bf16[2,400,256]{2,1,0:T(8,128)(2,1)S(1)}, bf16[2,400,256]{2,1,0:T(8,128)(2,1)S(1)}, u32[]{:S(2)}, u32[]{:S(2)}) %collective-permute-start.6) | collective-permute-done | bytes 409632 | tf_op jit(solution)/shard_map/ppermute | solution.py:563
  29.6 0.0 collective-permute-start.7
  29.6 4.4 %collective-permute-done.2.refs_3_ = bf16[2,400,256]{2,1,0:T(8,128)(2,1)S(1)} collective-permute-done((bf16[2,400,256]{2,1,0:T(8,128)(2,1)S(1)}, bf16[2,400,256]{2,1,0:T(8,128)(2,1)S(1)}, u32[]{:S(2)}, u32[]{:S(2)}) %collective-permute-start.2) | collective-permute-done | bytes 409632 | tf_op jit(solution)/shard_map/ppermute | solution.py:563
  33.9 1.9 collective-permute-start.10
  35.9 0.0 collective-permute-done.5.refs_6_
  35.9 2.5 collective-permute-done.3.refs_4_
  38.3 0.0 collective-permute-done.7.refs_8_
  38.4 2.0 collective-permute-start.11
  40.4 0.1 pad_add_fusion.refs_0_
  40.5 2.4 collective-permute-done.11.refs_12_
  42.9 49.7 %first_row_pass.1 = (f32[16,48,128]{2,1,0:T(8,128)S(1)}, s32[280]{0:T(512)S(1)}, f32[64,128]{1,0:T(8,128)S(1)}, f32[80,128]{1,0:T(8,128)S(1)}, bf16[16,384,256]{...) custom-call(s32[4]{0:T(128)S(1)} %pad_add_fusion.refs_0_, bf16[2,400,256]{2,1,0:T(8,128)(2,1)} %copy-done.2, ...), custom_call_target="tpu_custom_call" | custom-call | tf_op jit(solution)/shard_map/first_row_pass/pallas_call | solution.py:489
  92.6 17.0 %all_to_all.20.parts_ref = f32[16,48,128]{2,1,0:T(8,128)S(1)} all-to-all(f32[16,48,128]{2,1,0:T(8,128)S(1)} %get-tuple-element.27), channel_id=1, replica_groups=mesh['x'=4,'y'=4,'z'=4,'core'=2] {'y','z'}, dimensions={0} | all-to-all | bytes 786432 | tf_op jit(solution)/shard_map/all_to_all | solution.py:555
  109.6 39.1 %col_pass.1 = f32[8,64,128]{2,1,0:T(8,128)S(1)} custom-call(s32[280]{0:T(512)S(1)} %get-tuple-element.22.item_ref, bf16[16,384,256]{2,1,0:T(8,128)(2,1)S(1)} %get-tuple-element.23.x_ref, bf16[64,256,128]{2,1,0:T(8,128)(2,1)S(1)} %get-tuple-element.24.y_ref, f32[64,128]{1,0:T(8,128)S(1)} %get-tuple-element.25.side_ref, f32[16,48,128]{2,1,0:T(8,128)S(1)} %all_to_all.20.parts_ref), custom_call_target="tpu_custom_call" | custom-call | tf_op jit(solution)/shard_map/col_pass/pallas_call | solution.py:531
  148.6 15.3 %all_to_all.21.parts_ref = f32[8,64,128]{2,1,0:T(8,128)S(1)} all-to-all(f32[8,64,128]{2,1,0:T(8,128)S(1)} %col_pass.1), channel_id=1, replica_groups=mesh['x'=4,'y'=4,'z'=4,'core'=2] {'x','core'}, dimensions={0} | all-to-all | bytes 524288 | tf_op jit(solution)/shard_map/all_to_all | solution.py:555
  164.0 44.4 %row_pass.1 = f32[16,48,128]{2,1,0:T(8,128)S(1)} custom-call(s32[280]{0:T(512)S(1)} %get-tuple-element.22.item_ref, bf16[16,384,256]{2,1,0:T(8,128)(2,1)S(1)} %get-tuple-element.23.x_ref, bf16[64,256,128]{2,1,0:T(8,128)(2,1)S(1)} %get-tuple-element.24.y_ref, f32[80,128]{1,0:T(8,128)S(1)} %get-tuple-element.26.side_ref, f32[8,64,128]{2,1,0:T(8,128)S(1)} %all_to_all.21.parts_ref), custom_call_target="tpu_custom_call" | custom-call | tf_op jit(solution)/shard_map/row_pass/pallas_call | solution.py:519
  208.4 14.9 %all_to_all.22.parts_ref = f32[16,48,128]{2,1,0:T(8,128)S(1)} all-to-all(f32[16,48,128]{2,1,0:T(8,128)S(1)} %row_pass.1), channel_id=1, replica_groups=mesh['x'=4,'y'=4,'z'=4,'core'=2] {'y','z'}, dimensions={0} | all-to-all | bytes 786432 | tf_op jit(solution)/shard_map/all_to_all | solution.py:555
  223.3 39.5 %last_col_pass.1 = (f32[1,64,128]{2,1,0:T(8,128)S(1)}, f32[3,128]{1,0:T(4,128)}) custom-call(s32[280]{0:T(512)S(1)} %get-tuple-element.22.item_ref, bf16[16,384,256]{2,1,0:T(8,128)(2,1)S(1)} %get-tuple-element.23.x_ref, bf16[64,256,128]{2,1,0:T(8,128)(2,1)S(1)} %get-tuple-element.24.y_ref, f32[64,128]{1,0:T(8,128)S(1)} %get-tuple-element.25.side_ref, ...), custom_call_target="tpu_custom_call" | custom-call | tf_op jit(solution)/shard_map/last_col_pass/pallas_call | solution.py:543
  262.8 16.4 %all_to_all.23 = f32[8,8,128]{2,1,0:T(8,128)S(1)} all-to-all(f32[8,8,128]{2,1,0:T(8,128)S(1)} %bitcast.15), channel_id=1, replica_groups=mesh['x'=4,'y'=4,'z'=4,'core'=2] {'x','core'}, dimensions={0} | all-to-all | bytes 65536 | tf_op jit(solution)/shard_map/all_to_all | solution.py:555
  279.2 0.6 subtract_bitcast_fusion
  (35 shorter events, 0.1 us)
Async XLA Ops:
  3.1 8.7 %copy-start.11 = (bf16[400,256]{1,0:T(8,128)(2,1)S(1)}, bf16[400,256]{1,0:T(8,128)(2,1)}, u32[]{:S(2)}) copy-start(bf16[400,256]{1,0:T(8,128)(2,1)} %get-tuple-element.17) | copy-start | bytes 614404
  3.1 12.4 %collective-permute-start.8 = (bf16[8,272,128]{2,1,0:T(8,128)(2,1)}, bf16[8,272,128]{2,1,0:T(8,128)(2,1)S(1)}, u32[]{:S(2)}, u32[]{:S(2)}) collective-permute-start(bf16[8,272,128]{2,1,0:T(8,128)(2,1)} %get-tuple-element.18), channel_id=1, source_target_pairs={{0,32},{1,97},{2,34},{3,99},{4,36},{5,101},{6,38},{7,103},{8,40},{... | collective-permute-start | bytes 1671176 | tf_op jit(solution)/shard_map/ppermute | solution.py:563
  6.5 5.3 %collective-permute-start = (bf16[400,256]{1,0:T(8,128)(2,1)}, bf16[400,256]{1,0:T(8,128)(2,1)S(1)}, u32[]{:S(2)}, u32[]{:S(2)}) collective-permute-start(bf16[400,256]{1,0:T(8,128)(2,1)} %get-tuple-element.17), channel_id=1, source_target_pairs={{0,8},{1,3},{2,10},{3,1},{4,12},{5,7},{6,14},{7,5},{8,0},{9,11},{1... | collective-permute-start | bytes 614408 | tf_op jit(solution)/shard_map/ppermute | solution.py:563
  11.9 31.0 %copy-start.2 = (bf16[2,400,256]{2,1,0:T(8,128)(2,1)}, bf16[2,400,256]{2,1,0:T(8,128)(2,1)S(1)}, u32[]{:S(2)}) copy-start(bf16[2,400,256]{2,1,0:T(8,128)(2,1)S(1)} %pad_maximum_fusion.refs_1_) | copy-start | bytes 1228804
  11.9 9.3 %collective-permute-start.4 = (bf16[2,400,256]{2,1,0:T(8,128)(2,1)S(1)}, bf16[2,400,256]{2,1,0:T(8,128)(2,1)S(1)}, u32[]{:S(2)}, u32[]{:S(2)}) collective-permute-start(bf16[2,400,256]{2,1,0:T(8,128)(2,1)S(1)} %pad_maximum_fusion.refs_1_), channel_id=1, source_target_pairs={{0,24},{1,7},{2,26},{3,5},{4,28},{5,3},{6,30},{7,1},{8,16},{9,15},... | collective-permute-start | bytes 1228808 | tf_op jit(solution)/shard_map/ppermute | solution.py:563
  15.6 27.2 %copy-start.1 = (bf16[16,272,128]{2,1,0:T(8,128)(2,1)}, bf16[16,272,128]{2,1,0:T(8,128)(2,1)S(1)}, u32[]{:S(2)}) copy-start(bf16[16,272,128]{2,1,0:T(8,128)(2,1)S(1)} %constant_dynamic-update-slice_fusion.refs_9_) | copy-start | bytes 3342340
  15.6 22.7 %collective-permute-start.9 = (bf16[16,272,128]{2,1,0:T(8,128)(2,1)S(1)}, bf16[16,272,128]{2,1,0:T(8,128)(2,1)S(1)}, u32[]{:S(2)}, u32[]{:S(2)}) collective-permute-start(bf16[16,272,128]{2,1,0:T(8,128)(2,1)S(1)} %constant_dynamic-update-slice_fusion.refs_9_), channel_id=1, source_target_pairs={{0,96},{1,33},{2,98},{3,35},{4,100},{5,37},{6,102},{7,39},{8,104},... | collective-permute-start | bytes 3342344 | tf_op jit(solution)/shard_map/ppermute | solution.py:563
  15.7 8.2 %collective-permute-start.1 = (bf16[2,400,256]{2,1,0:T(8,128)(2,1)S(1)}, bf16[2,400,256]{2,1,0:T(8,128)(2,1)S(1)}, u32[]{:S(2)}, u32[]{:S(2)}) collective-permute-start(bf16[2,400,256]{2,1,0:T(8,128)(2,1)S(1)} %pad_maximum_fusion.refs_1_), channel_id=1, source_target_pairs={{0,2},{1,9},{2,0},{3,11},{4,6},{5,13},{6,4},{7,15},{8,10},{9,1},{1... | collective-permute-start | bytes 1228808 | tf_op jit(solution)/shard_map/ppermute | solution.py:563
  21.2 21.7 %copy-start.4 = (bf16[2,400,256]{2,1,0:T(8,128)(2,1)}, bf16[2,400,256]{2,1,0:T(8,128)(2,1)S(1)}, u32[]{:S(2)}) copy-start(bf16[2,400,256]{2,1,0:T(8,128)(2,1)S(1)} %collective-permute-done.4.refs_5_) | copy-start | bytes 1228804
  21.2 8.4 %collective-permute-start.6 = (bf16[2,400,256]{2,1,0:T(8,128)(2,1)S(1)}, bf16[2,400,256]{2,1,0:T(8,128)(2,1)S(1)}, u32[]{:S(2)}, u32[]{:S(2)}) collective-permute-start(bf16[2,400,256]{2,1,0:T(8,128)(2,1)S(1)} %collective-permute-done.4.refs_5_), channel_id=1, source_target_pairs={{0,6},{1,25},{2,4},{3,27},{4,2},{5,29},{6,0},{7,31},{8,14},{9,17},... | collective-permute-start | bytes 1228808 | tf_op jit(solution)/shard_map/ppermute | solution.py:563
  23.9 10.0 %collective-permute-start.2 = (bf16[2,400,256]{2,1,0:T(8,128)(2,1)S(1)}, bf16[2,400,256]{2,1,0:T(8,128)(2,1)S(1)}, u32[]{:S(2)}, u32[]{:S(2)}) collective-permute-start(bf16[2,400,256]{2,1,0:T(8,128)(2,1)S(1)} %pad_maximum_fusion.refs_1_), channel_id=1, source_target_pairs={{0,6},{1,25},{2,4},{3,27},{4,2},{5,29},{6,0},{7,31},{8,14},{9,17},... | collective-permute-start | bytes 1228808 | tf_op jit(solution)/shard_map/ppermute | solution.py:563
  24.0 11.9 %collective-permute-start.5 = (bf16[2,400,256]{2,1,0:T(8,128)(2,1)S(1)}, bf16[2,400,256]{2,1,0:T(8,128)(2,1)S(1)}, u32[]{:S(2)}, u32[]{:S(2)}) collective-permute-start(bf16[2,400,256]{2,1,0:T(8,128)(2,1)S(1)} %collective-permute-done.4.refs_5_), channel_id=1, source_target_pairs={{0,2},{1,9},{2,0},{3,11},{4,6},{5,13},{6,4},{7,15},{8,10},{9,1},{1... | collective-permute-start | bytes 1228808 | tf_op jit(solution)/shard_map/ppermute | solution.py:563
  24.0 18.9 %copy-start.5 = (bf16[2,400,256]{2,1,0:T(8,128)(2,1)}, bf16[2,400,256]{2,1,0:T(8,128)(2,1)S(1)}, u32[]{:S(2)}) copy-start(bf16[2,400,256]{2,1,0:T(8,128)(2,1)S(1)} %collective-permute-done.1.refs_2_) | copy-start | bytes 1228804
  24.0 14.4 %collective-permute-start.3 = (bf16[2,400,256]{2,1,0:T(8,128)(2,1)S(1)}, bf16[2,400,256]{2,1,0:T(8,128)(2,1)S(1)}, u32[]{:S(2)}, u32[]{:S(2)}) collective-permute-start(bf16[2,400,256]{2,1,0:T(8,128)(2,1)S(1)} %collective-permute-done.1.refs_2_), channel_id=1, source_target_pairs={{0,6},{1,25},{2,4},{3,27},{4,2},{5,29},{6,0},{7,31},{8,14},{9,17},... | collective-permute-start | bytes 1228808 | tf_op jit(solution)/shard_map/ppermute | solution.py:563
  29.6 8.8 %copy-start.6 = (bf16[2,400,256]{2,1,0:T(8,128)(2,1)}, bf16[2,400,256]{2,1,0:T(8,128)(2,1)S(1)}, u32[]{:S(2)}) copy-start(bf16[2,400,256]{2,1,0:T(8,128)(2,1)S(1)} %collective-permute-done.6.refs_7_) | copy-start | bytes 1228804
  29.6 8.8 %collective-permute-start.7 = (bf16[2,400,256]{2,1,0:T(8,128)(2,1)S(1)}, bf16[2,400,256]{2,1,0:T(8,128)(2,1)S(1)}, u32[]{:S(2)}, u32[]{:S(2)}) collective-permute-start(bf16[2,400,256]{2,1,0:T(8,128)(2,1)S(1)} %collective-permute-done.6.refs_7_), channel_id=1, source_target_pairs={{0,2},{1,9},{2,0},{3,11},{4,6},{5,13},{6,4},{7,15},{8,10},{9,1},{1... | collective-permute-start | bytes 1228808 | tf_op jit(solution)/shard_map/ppermute | solution.py:563
  33.9 6.4 %copy-start.7 = (bf16[2,400,256]{2,1,0:T(8,128)(2,1)}, bf16[2,400,256]{2,1,0:T(8,128)(2,1)S(1)}, u32[]{:S(2)}) copy-start(bf16[2,400,256]{2,1,0:T(8,128)(2,1)S(1)} %collective-permute-done.2.refs_3_) | copy-start | bytes 1228804
  33.9 6.5 %collective-permute-start.10 = (bf16[16,272,128]{2,1,0:T(8,128)(2,1)S(1)}, bf16[16,272,128]{2,1,0:T(8,128)(2,1)}, u32[]{:S(2)}, u32[]{:S(2)}) collective-permute-start(bf16[16,272,128]{2,1,0:T(8,128)(2,1)S(1)} %constant_dynamic-update-slice_fusion.refs_9_), channel_id=1, source_target_pairs={{0,1},{1,0},{2,3},{3,2},{4,5},{5,4},{6,7},{7,6},{8,9},{9,8},{10,11... | collective-permute-start | bytes 3342344 | tf_op jit(solution)/shard_map/ppermute | solution.py:563
  35.9 4.5 %copy-start.8 = (bf16[2,400,256]{2,1,0:T(8,128)(2,1)}, bf16[2,400,256]{2,1,0:T(8,128)(2,1)S(1)}, u32[]{:S(2)}) copy-start(bf16[2,400,256]{2,1,0:T(8,128)(2,1)S(1)} %collective-permute-done.5.refs_6_) | copy-start | bytes 1228804
  38.3 2.0 copy-start.9
  38.3 2.0 copy-start.10
  38.4 4.5 %copy-start.3 = (bf16[16,272,128]{2,1,0:T(8,128)(2,1)}, bf16[16,272,128]{2,1,0:T(8,128)(2,1)S(1)}, u32[]{:S(2)}) copy-start(bf16[16,272,128]{2,1,0:T(8,128)(2,1)S(1)} %collective-permute-done.9.refs_10_) | copy-start | bytes 3342340
  38.4 4.5 %collective-permute-start.11 = (bf16[16,272,128]{2,1,0:T(8,128)(2,1)S(1)}, bf16[16,272,128]{2,1,0:T(8,128)(2,1)}, u32[]{:S(2)}, u32[]{:S(2)}) collective-permute-start(bf16[16,272,128]{2,1,0:T(8,128)(2,1)S(1)} %collective-permute-done.9.refs_10_), channel_id=1, source_target_pairs={{0,1},{1,0},{2,3},{3,2},{4,5},{5,4},{6,7},{7,6},{8,9},{9,8},{10,11... | collective-permute-start | bytes 3342344 | tf_op jit(solution)/shard_map/ppermute | solution.py:563
  164.0 59.3 %copy-start = (f32[3,128]{1,0:T(4,128)S(1)}, f32[3,128]{1,0:T(4,128)}, u32[]{:S(2)}) copy-start(f32[3,128]{1,0:T(4,128)} %get-tuple-element.28.norm_ref) | copy-start | bytes 4612
  223.3 55.9 %copy-start.12 = (f32[8,128]{1,0:T(8,128)S(1)}, f32[8,128]{1,0:T(8,128)}, u32[]{:S(2)}) copy-start(f32[8,128]{1,0:T(8,128)} %get-tuple-element.30) | copy-start | bytes 12292
